TPU v7x, 32 devices: a whole 2x2x4 slice. The times are simulated.
32 devices in a mesh: row: 4 (over y, x), col: 2 (over core), depth: 4 (over z).
Axes of the slice: x: 2, y: 2, z: 4, core: 2. Of those that a mesh axis runs over, the one named last changes fastest.
Arguments:
- x_vals: bfloat16 [4, 16, 4, 128, 128], P('row', ('col', 'depth')), may hold values from -2.5 to 2.5
- x_rows: int32 [4, 16, 4], P('row', ('col', 'depth')), may hold values from -1 to 3, as said below
- out_block: int32 [4, 2, 4], P('row', 'col', 'depth'), may hold values from 0 to 15, as said below
Outputs:
- product_blocks: bfloat16 [4, 2, 4, 128, 128], P('row', 'col', 'depth')
Inputs may be any that keep to these rules, and one draw needn't show every extreme that they name: `x_rows`: within one row group and block column the filled slots name distinct rows. In every row group, each run of 2 block columns that starts at a multiple of 2 has a column with all 4 slots filled. `out_block`: within one tile the 4 entries are distinct positions, and every tile lists position 15 among them.
All inputs are finite; a program needn't handle non-finite values.
Results may differ from a plain program's by a relative error of at most 0.001.
Values may be sent and summed in bfloat16 or wider, within the bound.
A program may use at most 128 MiB of HBM per device.

v0:
```python
import jax
import jax.numpy as jnp
from jax import lax
from jax.sharding import PartitionSpec as P


def shifted(value, axis, steps):
    count = lax.axis_size(axis)
    pairs = [(source, (source + steps) % count) for source in range(count)]
    return lax.ppermute(value, axis, pairs)


def accumulate(partial_value, operands, positions, group_rows):
    left_vals, left_rows, right_vals, right_rows = operands
    slot_total = left_vals.shape[0] * left_vals.shape[1]
    left_valid = left_rows >= 0
    for slot_index in range(right_vals.shape[1]):
        partner_slot = right_vals[:, slot_index]
        right_slot_rows = right_rows[:, slot_index]
        blocks = jnp.einsum(
            "ksab,kcb->ksac", left_vals, partner_slot, preferred_element_type=jnp.float32
        )
        target = left_rows * group_rows + right_slot_rows[:, None]
        target = jnp.where(left_valid & (right_slot_rows >= 0)[:, None], target, -1)
        select = (target.reshape(1, slot_total) == positions[:, None]).astype(jnp.float32)
        gained = jnp.dot(
            select,
            blocks.reshape(slot_total, -1),
            precision=lax.Precision.HIGHEST,
            preferred_element_type=jnp.float32,
        )
        partial_value = partial_value + gained.reshape(partial_value.shape)
    return partial_value


def on_device(x_vals, x_rows, out_block):
    row_count = lax.axis_size("row")
    col_count = lax.axis_size("col")
    depth_count = lax.axis_size("depth")
    col_index = lax.axis_index("col")
    midpoint = col_count // 2
    group_rows = x_vals.shape[1] * col_count * depth_count // row_count
    positions = lax.all_gather(out_block, "depth", axis=2, tiled=True).reshape(-1)
    home_vals = x_vals[0]
    home_rows = x_rows[0]
    partial_value = jnp.zeros((positions.shape[0],) + x_vals.shape[3:], jnp.float32)
    up_count = jnp.maximum(midpoint - col_index, 0)
    down_count = jnp.maximum(col_index - midpoint, 0)
    partner_vals, partner_rows = (home_vals, home_rows)
    for round_number in range(midpoint):
        arrived = shifted((partner_vals, partner_rows), "row", 1)
        use_moved = round_number < up_count
        partner_vals = jnp.where(use_moved, arrived[0], partner_vals)
        partner_rows = jnp.where(use_moved, arrived[1], partner_rows)
    for round_number in range(col_count - 1 - midpoint):
        arrived = shifted((partner_vals, partner_rows), "row", -1)
        use_moved = round_number < down_count
        partner_vals = jnp.where(use_moved, arrived[0], partner_vals)
        partner_rows = jnp.where(use_moved, arrived[1], partner_rows)
    operands = (home_vals, home_rows, partner_vals, partner_rows)
    partial_value = accumulate(partial_value, operands, positions, group_rows)
    at_first = col_index == 0
    current = operands
    for round_number in range(1, col_count):
        arrived = shifted((current[2], current[3]), "row", 1)
        wrapped = shifted((current[2], current[3]), "row", 1 - col_count)
        moved_vals = jnp.where(at_first, wrapped[0], arrived[0])
        moved_rows = jnp.where(at_first, wrapped[1], arrived[1])
        current = shifted((current[0], current[1], moved_vals, moved_rows), "col", -1)
        partial_value = accumulate(partial_value, current, positions, group_rows)
    summed = lax.psum_scatter(partial_value, "depth", scatter_dimension=0, tiled=True)
    return summed.astype(jnp.bfloat16).reshape(out_block.shape + x_vals.shape[3:])


def solution(mesh):
    in_specs = (
        P("row", ("col", "depth"), None, None, None),
        P("row", ("col", "depth"), None),
        P("row", "col", "depth"),
    )
    out_specs = P("row", "col", "depth", None, None)
    return jax.shard_map(
        on_device, mesh=mesh, in_specs=in_specs, out_specs=out_specs, check_vma=False
    )
```

profile of v0, /device:TPU:0, one launch (start us, length us, event | category | flops | bytes accessed | tf_op | source)
XLA Modules:
  0.0 79.1 jit_solution(6080923275031557147)
XLA Ops:
  6.5 1.0 %copy.111 = bf16[1,2,4,128,128]{4,3,1,2,0:T(8,128)(2,1)S(1)} copy(bf16[1,2,4,128,128]{4,3,2,1,0:T(8,128)(2,1)} %param.3) | data formatting | bytes 524288 | tf_op args[0]
  7.6 3.0 %collective-permute-start.1 = (bf16[2,4,128,128]{3,2,0,1:T(8,128)(2,1)S(1)}, bf16[2,4,128,128]{3,2,0,1:T(8,128)(2,1)S(1)}, u32[]{:S(2)}, u32[]{:S(2)}) collective-permute-start(bf16[2,4,128,128]{3,2,0,1:T(8,128)(2,1)S(1)} %bitcast.200), channel_id=1, source_target_pairs={{0,8},{8,16},{16,24},{24,0},{1,9},{9,17},{17,25},{25,1},{2,10},{10... | collective-permute-start | bytes 786440 | tf_op jit(solution)/shard_map/ppermute | solution.py:10
  10.6 1.5 %collective-permute-start = (s32[2,4]{1,0:T(2,128)S(1)}, s32[2,4]{1,0:T(2,128)S(1)}, u32[]{:S(2)}, u32[]{:S(2)}) collective-permute-start(s32[2,4]{1,0:T(2,128)S(1)} %bitcast.202), channel_id=1, source_target_pairs={{0,8},{8,16},{16,24},{24,0},{1,9},{9,17},{17,25},{25,1},{2,10},{10... | collective-permute-start | bytes 104 | tf_op jit(solution)/shard_map/ppermute | solution.py:10
  12.1 0.2 collective-permute-start.2
  12.3 0.1 ge.55
  13.1 0.6 dynamic-slice
  13.7 0.7 bitcast_dynamic-update-slice_fusion
  14.3 0.1 mul.29
  14.4 8.4 %all-reduce = s32[4]{0:T(128)S(1)} all-reduce(s32[4]{0:T(128)S(1)} %bitcast_dynamic-update-slice_fusion), channel_id=1, replica_groups=mesh['row'=4,'col'=2,'depth'=4] {'depth'}, use_global_device_ids=true, to_apply=%add | all-reduce | flops 4 | bytes 32
  22.9 0.2 compare_reduce_fusion.4
  23.1 0.2 slice_reduce_fusion.4
  23.3 1.5 %collective-permute-start.3 = (s32[2,4]{1,0:T(2,128)S(1)}, s32[2,4]{1,0:T(2,128)S(1)}, u32[]{:S(2)}, u32[]{:S(2)}) collective-permute-start(s32[2,4]{1,0:T(2,128)S(1)} %broadcast_select_fusion.3), channel_id=1, source_target_pairs={{0,24},{8,0},{16,8},{24,16},{1,25},{9,1},{17,9},{25,17},{2,26},{10... | collective-permute-start | bytes 104 | tf_op jit(solution)/shard_map/ppermute | solution.py:10
  24.8 0.6 collective-permute-start.4
  25.4 0.1 and.118
  25.5 0.1 and.119
  25.6 0.1 add.143
  25.8 0.1 add.138
  25.9 0.1 and.115
  26.1 0.1 add.133
  26.3 0.1 and.111
  26.4 0.1 add.129
  26.6 0.1 and.107
  26.7 0.3 collective-permute-done.3
  26.9 2.3 %collective-permute-done.4 = s32[2,4]{1,0:T(2,128)S(1)} collective-permute-done((s32[2,4]{1,0:T(2,128)S(1)}, s32[2,4]{1,0:T(2,128)S(1)}, u32[]{:S(2)}, u32[]{:S(2)}) %collective-permute-start.4) | collective-permute-done | bytes 64 | tf_op jit(solution)/shard_map/ppermute | solution.py:10
  29.3 1.1 %collective-permute-done.5 = s32[2,4]{1,0:T(2,128)S(1)} collective-permute-done((s32[2,4]{1,0:T(2,128)S(1)}, s32[2,4]{1,0:T(2,128)S(1)}, u32[]{:S(2)}, u32[]{:S(2)}) %collective-permute-start.5) | collective-permute-done | bytes 64 | tf_op jit(solution)/shard_map/ppermute | solution.py:10
  30.4 0.2 compare_reduce_fusion
  30.6 0.2 slice_reduce_fusion
  30.9 0.1 and_select_fusion
  30.9 0.1 eq.114
  31.0 0.1 eq.117
  31.1 0.1 eq.120
  31.2 0.1 eq.123
  31.3 0.2 convolution_bitcast_fusion.7
  31.5 0.2 convolution_bitcast_fusion.6
  31.8 0.1 collective-permute-start.6
  31.9 2.0 %collective-permute-start.7 = (bf16[2,4,128,128]{3,2,0,1:T(8,128)(2,1)S(1)}, bf16[2,4,128,128]{3,2,0,1:T(8,128)(2,1)S(1)}, u32[]{:S(2)}, u32[]{:S(2)}) collective-permute-start(bf16[2,4,128,128]{3,2,0,1:T(8,128)(2,1)S(1)} %broadcast_select_fusion.1), channel_id=1, source_target_pairs={{0,8},{8,16},{16,24},{24,0},{1,9},{9,17},{17,25},{25,1},{2,10},{10... | collective-permute-start | bytes 786440 | tf_op jit(solution)/shard_map/ppermute | solution.py:10
  33.9 0.2 copy.32
  34.1 0.2 copy.34
  34.3 0.7 fusion.7
  34.9 0.7 convolution_add_fusion.6
  35.6 0.2 convolution_bitcast_fusion.5
  35.8 0.2 copy.36
  36.0 0.7 convolution_add_fusion.5
  36.7 4.3 %collective-permute-done.6 = bf16[2,4,128,128]{3,2,0,1:T(8,128)(2,1)S(1)} collective-permute-done((bf16[2,4,128,128]{3,2,0,1:T(8,128)(2,1)S(1)}, bf16[2,4,128,128]{3,2,0,1:T(8,128)(2,1)S(1)}, u32[]{:S(2)}, u32[]{:S(2)}) %collective-permute-start.6) | collective-permute-done | bytes 262176 | tf_op jit(solution)/shard_map/ppermute | solution.py:10
  41.0 5.8 %collective-permute-done.7 = bf16[2,4,128,128]{3,2,0,1:T(8,128)(2,1)S(1)} collective-permute-done((bf16[2,4,128,128]{3,2,0,1:T(8,128)(2,1)S(1)}, bf16[2,4,128,128]{3,2,0,1:T(8,128)(2,1)S(1)}, u32[]{:S(2)}, u32[]{:S(2)}) %collective-permute-start.7) | collective-permute-done | bytes 262176 | tf_op jit(solution)/shard_map/ppermute | solution.py:10
  46.9 0.2 convolution_bitcast_fusion.4
  47.2 0.2 copy.38
  47.4 0.7 convolution_add_fusion.4
  48.0 0.4 collective-permute-done.8
  48.4 0.2 convolution_bitcast_fusion.3
  48.7 0.2 copy.40
  48.9 0.2 convolution_bitcast_fusion.2
  49.1 0.2 copy.42
  49.3 0.2 convolution_bitcast_fusion.1
  49.6 0.2 copy.44
  49.8 0.2 convolution_bitcast_fusion
  50.0 0.2 copy.46
  50.2 0.7 convolution_add_fusion.3
  50.9 0.7 convolution_add_fusion.2
  51.5 0.7 convolution_add_fusion.1
  52.2 0.7 convolution_add_fusion
  52.9 0.7 copy.47
  53.6 17.1 %reduce-scatter.2.cloned.1.call-done = f32[1,128,128]{2,1,0:T(8,128)} async-done(((f32[4,128,128]{2,1,0:T(8,128)}), f32[1,128,128]{2,1,0:T(8,128)}) %reduce-scatter.2.cloned.1.call-update) | async-done | bytes 65552 | tf_op jit(solution)/shard_map/reduce_scatter | solution.py:71
  70.8 1.5 %convert_bitcast_fusion = bf16[1,1,1,128,128]{4,3,2,1,0:T(8,128)(2,1)} fusion(f32[1,128,128]{2,1,0:T(8,128)} %reduce-scatter.2.cloned.1.call-done), kind=kLoop, calls=%fused_computation.51 | loop fusion | flops 16384 | bytes 98304 | tf_op jit(solution)/shard_map/reshape | solution.py:72
  (30 shorter events, 0.7 us)
Async XLA Ops:
  6.5 24.7 %copy-start = (bf16[1,2,4,128,128]{4,3,2,1,0:T(8,128)(2,1)S(1)}, bf16[1,2,4,128,128]{4,3,2,1,0:T(8,128)(2,1)}, u32[]{:S(2)}) copy-start(bf16[1,2,4,128,128]{4,3,2,1,0:T(8,128)(2,1)} %param.3) | copy-start | bytes 786436
  6.5 64.2 %reduce-scatter.2.cloned.1.call-start = ((), (), s32[]{:S(2)}) async-start(), calls=%async_computation.1 | async-start | bytes 327680 | tf_op jit(solution)/shard_map/reduce_scatter | solution.py:71
  7.6 3.0 %copy-start.1 = (s32[1,2,4]{2,1,0:T(2,128)S(1)}, s32[1,2,4]{2,1,0:T(2,128)}, u32[]{:S(2)}) copy-start(s32[1,2,4]{2,1,0:T(2,128)} %param.4) | copy-start | bytes 100
  7.6 23.7 %collective-permute-start.1 = (bf16[2,4,128,128]{3,2,0,1:T(8,128)(2,1)S(1)}, bf16[2,4,128,128]{3,2,0,1:T(8,128)(2,1)S(1)}, u32[]{:S(2)}, u32[]{:S(2)}) collective-permute-start(bf16[2,4,128,128]{3,2,0,1:T(8,128)(2,1)S(1)} %bitcast.200), channel_id=1, source_target_pairs={{0,8},{8,16},{16,24},{24,0},{1,9},{9,17},{17,25},{25,1},{2,10},{10... | collective-permute-start | bytes 786440 | tf_op jit(solution)/shard_map/ppermute | solution.py:10
  10.6 37.5 %collective-permute-start.9 = (bf16[2,4,128,128]{3,2,0,1:T(8,128)(2,1)S(1)}, bf16[2,4,128,128]{3,2,0,1:T(8,128)(2,1)S(1)}, u32[]{:S(2)}, u32[]{:S(2)}) collective-permute-start(bf16[2,4,128,128]{3,2,0,1:T(8,128)(2,1)S(1)} %bitcast.201), channel_id=1, source_target_pairs={{0,4},{4,0},{1,5},{5,1},{2,6},{6,2},{3,7},{7,3},{8,12},{12,8},{9,1... | collective-permute-start | bytes 786440 | tf_op jit(solution)/shard_map/ppermute | solution.py:10
  10.6 12.3 %collective-permute-start = (s32[2,4]{1,0:T(2,128)S(1)}, s32[2,4]{1,0:T(2,128)S(1)}, u32[]{:S(2)}, u32[]{:S(2)}) collective-permute-start(s32[2,4]{1,0:T(2,128)S(1)} %bitcast.202), channel_id=1, source_target_pairs={{0,8},{8,16},{16,24},{24,0},{1,9},{9,17},{17,25},{25,1},{2,10},{10... | collective-permute-start | bytes 104 | tf_op jit(solution)/shard_map/ppermute | solution.py:10
  12.1 18.8 %collective-permute-start.2 = (s32[2,4]{1,0:T(2,128)S(1)}, s32[2,4]{1,0:T(2,128)S(1)}, u32[]{:S(2)}, u32[]{:S(2)}) collective-permute-start(s32[2,4]{1,0:T(2,128)S(1)} %bitcast.203), channel_id=1, source_target_pairs={{0,4},{4,0},{1,5},{5,1},{2,6},{6,2},{3,7},{7,3},{8,12},{12,8},{9,1... | collective-permute-start | bytes 104 | tf_op jit(solution)/shard_map/ppermute | solution.py:10
  12.4 0.7 copy-start.2
  23.3 3.6 %collective-permute-start.3 = (s32[2,4]{1,0:T(2,128)S(1)}, s32[2,4]{1,0:T(2,128)S(1)}, u32[]{:S(2)}, u32[]{:S(2)}) collective-permute-start(s32[2,4]{1,0:T(2,128)S(1)} %broadcast_select_fusion.3), channel_id=1, source_target_pairs={{0,24},{8,0},{16,8},{24,16},{1,25},{9,1},{17,9},{25,17},{2,26},{10... | collective-permute-start | bytes 104 | tf_op jit(solution)/shard_map/ppermute | solution.py:10
  24.8 4.5 %collective-permute-start.4 = (s32[2,4]{1,0:T(2,128)S(1)}, s32[2,4]{1,0:T(2,128)S(1)}, u32[]{:S(2)}, u32[]{:S(2)}) collective-permute-start(s32[2,4]{1,0:T(2,128)S(1)} %broadcast_select_fusion.3), channel_id=1, source_target_pairs={{0,8},{8,16},{16,24},{24,0},{1,9},{9,17},{17,25},{25,1},{2,10},{10... | collective-permute-start | bytes 104 | tf_op jit(solution)/shard_map/ppermute | solution.py:10
  29.3 1.1 %collective-permute-start.5 = (s32[2,4]{1,0:T(2,128)S(1)}, s32[2,4]{1,0:T(2,128)S(1)}, u32[]{:S(2)}, u32[]{:S(2)}) collective-permute-start(s32[2,4]{1,0:T(2,128)S(1)} %broadcast_select_fusion.2), channel_id=1, source_target_pairs={{0,4},{4,0},{1,5},{5,1},{2,6},{6,2},{3,7},{7,3},{8,12},{12,8},{9,1... | collective-permute-start | bytes 104 | tf_op jit(solution)/shard_map/ppermute | solution.py:10
  31.8 9.2 %collective-permute-start.6 = (bf16[2,4,128,128]{3,2,0,1:T(8,128)(2,1)S(1)}, bf16[2,4,128,128]{3,2,0,1:T(8,128)(2,1)S(1)}, u32[]{:S(2)}, u32[]{:S(2)}) collective-permute-start(bf16[2,4,128,128]{3,2,0,1:T(8,128)(2,1)S(1)} %broadcast_select_fusion.1), channel_id=1, source_target_pairs={{0,24},{8,0},{16,8},{24,16},{1,25},{9,1},{17,9},{25,17},{2,26},{10... | collective-permute-start | bytes 786440 | tf_op jit(solution)/shard_map/ppermute | solution.py:10
  31.9 14.9 %collective-permute-start.7 = (bf16[2,4,128,128]{3,2,0,1:T(8,128)(2,1)S(1)}, bf16[2,4,128,128]{3,2,0,1:T(8,128)(2,1)S(1)}, u32[]{:S(2)}, u32[]{:S(2)}) collective-permute-start(bf16[2,4,128,128]{3,2,0,1:T(8,128)(2,1)S(1)} %broadcast_select_fusion.1), channel_id=1, source_target_pairs={{0,8},{8,16},{16,24},{24,0},{1,9},{9,17},{17,25},{25,1},{2,10},{10... | collective-permute-start | bytes 786440 | tf_op jit(solution)/shard_map/ppermute | solution.py:10
  46.8 1.6 %collective-permute-start.8 = (bf16[2,4,128,128]{3,2,0,1:T(8,128)(2,1)S(1)}, bf16[2,4,128,128]{3,2,0,1:T(8,128)(2,1)S(1)}, u32[]{:S(2)}, u32[]{:S(2)}) collective-permute-start(bf16[2,4,128,128]{3,2,0,1:T(8,128)(2,1)S(1)} %broadcast_select_fusion), channel_id=1, source_target_pairs={{0,4},{4,0},{1,5},{5,1},{2,6},{6,2},{3,7},{7,3},{8,12},{12,8},{9,1... | collective-permute-start | bytes 786440 | tf_op jit(solution)/shard_map/ppermute | solution.py:10
Sparse Core Ops, SparseCore 0:
  53.7 16.9 reduce-scatter.1
where the time goes:
time: 79.3 us; the launch traced here: 79.1 us
  waiting for transfers between devices  31.4 us (40%)
  between operations  14.3 us (18%)
  starting transfers between devices  8.94 us (11%)
  blocking collectives  8.44 us (11%)
  matrix products  7.13 us (9%)
  local copies, waits for them, and re-layouts  6.77 us (9%)
  other arithmetic  2.06 us (3%)
    reduce_scatter x1, waiting for transfers between devices, on_device(): lax.psum_scatter(partial_value, 'depth', scatter_dimension=0, tiled=True)  17.1 us
    ppermute x10, waiting for transfers between devices, shifted(): return lax.ppermute(value, axis, pairs)  14.2 us
    ppermute x10, starting transfers between devices, shifted(): return lax.ppermute(value, axis, pairs)  8.94 us
    unnamed x1, blocking collectives  8.44 us
    dot_general x8, matrix products, accumulate(): jnp.dot(select, blocks.reshape(slot_total, -1), precision=lax.Precision.H...  5.33 us
    unnamed x10, local copies, waits for them, and re-layouts  2.31 us
    dot_general x8, matrix products, accumulate(): jnp.einsum('ksab,kcb->ksac', left_vals, partner_slot, preferred_element_t...  1.8 us
  transfers between devices with their start and end apart: 11, of which 7 were waited for; matrix products, arithmetic and copies ran while one was open for 11% of the time, Pallas kernels for 0%

commit v1 on v0

v1 whole, which is shorter than its diff:
```python
import functools

import jax
import jax.numpy as jnp
from jax import lax
from jax.experimental import pallas as pl
from jax.experimental.pallas import tpu as pltpu
from jax.sharding import PartitionSpec as P

MESH = pl.DeviceIdType.MESH


def product(left, right):
    return lax.dot_general(
        left, right, (((1,), (1,)), ((), ())), preferred_element_type=jnp.float32
    )


def kernel(
    sizes, rows_ref, pos_ref, x_ref, out_ref,
    raw, home, partner, pos_vmem, pos_smem, send_parts, recv_parts,
    local_sem, home_send, home_recv, partner_send, partner_recv,
    pos_send, pos_recv, sum_send, sum_recv,
):
    row_count, col_count, depth_count = sizes
    width, slots, size = x_ref.shape[1], x_ref.shape[2], x_ref.shape[3]
    group_rows = home.shape[1]
    midpoint = col_count // 2
    row, col, depth = (lax.axis_index(name) for name in ("row", "col", "depth"))
    has_partner = col != midpoint

    def place(row_index, col_index, depth_index):
        return {"row": row_index, "col": col_index, "depth": depth_index}

    load = pltpu.make_async_copy(x_ref.at[0], raw, local_sem.at[0])
    load.start()

    barrier = pltpu.get_barrier_semaphore()

    def greet(device):
        pl.semaphore_signal(barrier, inc=1, device_id=device, device_id_type=MESH)

    for step in range(1, col_count):
        greet(place(row, lax.rem(col + step, col_count), depth))
    for step in range(1, depth_count):
        greet(place(row, col, lax.rem(depth + step, depth_count)))

    @pl.when(has_partner)
    def _():
        source_row = lax.rem(row + col - midpoint + row_count, row_count)
        for step in range(col_count):
            greet(place(source_row, lax.rem(col + step, col_count), depth))

    pos_vmem[0] = jnp.full(pos_vmem.shape[1:], pos_ref[0, 0, 0], jnp.int32)
    load.wait()
    for column in range(width):
        for block_row in range(group_rows):
            slot = jnp.int32(0)
            found = jnp.int32(0)
            for index in range(slots):
                match = rows_ref[0, column, index] == block_row
                slot = jnp.where(match, index, slot)
                found = jnp.where(match, 1, found)
            block = raw[column, slot]
            home[0, block_row, :, column * size:(column + 1) * size] = jnp.where(
                found > 0, block, jnp.zeros_like(block)
            )

    pl.semaphore_wait(barrier, 2 * (col_count - 1) + depth_count - 1)

    def home_copy(step):
        return pltpu.make_async_remote_copy(
            src_ref=home.at[0],
            dst_ref=home.at[step],
            send_sem=home_send.at[step],
            recv_sem=home_recv.at[step],
            device_id=place(row, lax.rem(col + step, col_count), depth),
            device_id_type=MESH,
        )

    def partner_copy(step):
        target_col = lax.rem(col + step, col_count)
        target_row = lax.rem(row + midpoint - target_col + row_count, row_count)
        return pltpu.make_async_remote_copy(
            src_ref=home.at[0],
            dst_ref=partner.at[step],
            send_sem=partner_send.at[step],
            recv_sem=partner_recv.at[step],
            device_id=place(target_row, target_col, depth),
            device_id_type=MESH,
        )

    def pos_copy(step):
        return pltpu.make_async_remote_copy(
            src_ref=pos_vmem.at[0],
            dst_ref=pos_vmem.at[step],
            send_sem=pos_send.at[step],
            recv_sem=pos_recv.at[step],
            device_id=place(row, col, lax.rem(depth + step, depth_count)),
            device_id_type=MESH,
        )

    def sum_copy(step):
        return pltpu.make_async_remote_copy(
            src_ref=send_parts.at[step],
            dst_ref=recv_parts.at[step],
            send_sem=sum_send.at[step],
            recv_sem=sum_recv.at[step],
            device_id=place(row, col, lax.rem(depth + step, depth_count)),
            device_id_type=MESH,
        )

    def sends_partner(step):
        return lax.rem(col + step, col_count) != midpoint

    for step in range(col_count):
        pl.when(sends_partner(step))(lambda: partner_copy(step).start())
        if step:
            home_copy(step).start()
    for step in range(1, depth_count):
        pos_copy(step).start()

    for step in range(1, depth_count):
        pos_copy(step).wait_recv()
    listed = pltpu.make_async_copy(pos_vmem, pos_smem, local_sem.at[1])
    listed.start()
    listed.wait()
    for step in range(1, col_count):
        home_copy(step).wait_recv()

    def one_entry(right, step):
        position = pos_smem[(depth_count - step) % depth_count, 0, 0]
        left_row = lax.div(position, group_rows)
        right_row = lax.rem(position, group_rows)
        total = product(home[0, left_row], right[0, right_row])
        for index in range(1, col_count):
            total = total + product(home[index, left_row], right[index, right_row])
        return total

    def tile(right):
        for step in range(1, depth_count):
            send_parts[step] = one_entry(right, step)
            sum_copy(step).start()
        send_parts[0] = one_entry(right, 0)

    @pl.when(has_partner)
    def _():
        for step in range(col_count):
            partner_copy(step).wait_recv()
        tile(partner)

    @pl.when(jnp.logical_not(has_partner))
    def _():
        tile(home)

    total = send_parts[0]
    for step in range(1, depth_count):
        sum_copy(step).wait_recv()
        total = total + recv_parts[step]
    out_ref[0, 0, 0] = total.astype(out_ref.dtype)

    for step in range(col_count):
        pl.when(sends_partner(step))(lambda: partner_copy(step).wait_send())
        if step:
            home_copy(step).wait_send()
    for step in range(1, depth_count):
        pos_copy(step).wait_send()
        sum_copy(step).wait_send()


def on_device(sizes, x_vals, x_rows, out_block):
    row_count, col_count, depth_count = sizes
    _, width, slots, size, _ = x_vals.shape
    group_rows = width * col_count * depth_count // row_count
    dma = pltpu.SemaphoreType.DMA
    return pl.pallas_call(
        functools.partial(kernel, sizes),
        out_shape=jax.ShapeDtypeStruct(out_block.shape + (size, size), jnp.bfloat16),
        in_specs=[
            pl.BlockSpec(memory_space=pltpu.SMEM),
            pl.BlockSpec(memory_space=pltpu.SMEM),
            pl.BlockSpec(memory_space=pl.ANY),
        ],
        out_specs=pl.BlockSpec(memory_space=pltpu.VMEM),
        scratch_shapes=[
            pltpu.VMEM((width, slots, size, size), x_vals.dtype),
            pltpu.VMEM((col_count, group_rows, size, width * size), x_vals.dtype),
            pltpu.VMEM((col_count, group_rows, size, width * size), x_vals.dtype),
            pltpu.VMEM((depth_count, 8, 128), jnp.int32),
            pltpu.SMEM((depth_count, 8, 128), jnp.int32),
            pltpu.VMEM((depth_count, size, size), jnp.float32),
            pltpu.VMEM((depth_count, size, size), jnp.float32),
            dma((2,)),
            dma((col_count,)),
            dma((col_count,)),
            dma((col_count,)),
            dma((col_count,)),
            dma((depth_count,)),
            dma((depth_count,)),
            dma((depth_count,)),
            dma((depth_count,)),
        ],
        compiler_params=pltpu.CompilerParams(collective_id=0, has_side_effects=True),
    )(x_rows, out_block, x_vals)


def solution(mesh):
    sizes = tuple(mesh.shape[name] for name in ("row", "col", "depth"))
    in_specs = (
        P("row", ("col", "depth"), None, None, None),
        P("row", ("col", "depth"), None),
        P("row", "col", "depth"),
    )
    out_specs = P("row", "col", "depth", None, None)
    return jax.shard_map(
        functools.partial(on_device, sizes),
        mesh=mesh, in_specs=in_specs, out_specs=out_specs, check_vma=False,
    )
```

time: 79.3 us -> 22 us (0.28)
  waiting for transfers between devices: 31.4 us -> 0 us
  Pallas kernels: 0 us -> 19.8 us
  between operations: 14.3 us -> 0.66 us
  starting transfers between devices: 8.94 us -> 0 us
  blocking collectives: 8.44 us -> 0 us
  matrix products: 7.13 us -> 0 us
  local copies, waits for them, and re-layouts: 6.77 us -> 1.38 us
  other arithmetic: 2.06 us -> 0 us
    pallas_call x0 -> x1, Pallas kernels: none -> 19.8 us  [on_device(): pl.pallas_call(functools.partial(kernel, sizes), out_shape=jax.ShapeDtype...]
    reduce_scatter x1 -> x0, waiting for transfers between devices: 17.1 us -> none  [on_device(): lax.psum_scatter(partial_value, 'depth', scatter_dimension=0, tiled=True)]
    ppermute x10 -> x0, waiting for transfers between devices: 14.2 us -> none  [shifted(): return lax.ppermute(value, axis, pairs)]
    ppermute x10 -> x0, starting transfers between devices: 8.94 us -> none  [shifted(): return lax.ppermute(value, axis, pairs)]
    unnamed x1 -> x0, blocking collectives: 8.44 us -> none
    dot_general x16 -> x0, matrix products: 7.13 us -> none  [the longest x8 5.33 us: accumulate(): jnp.dot(select, blocks.reshape(slot_total, -1), precision=lax.Precision.H...]
    dot_general x8 -> x0, local copies, waits for them, and re-layouts: 1.57 us -> none  [accumulate(): jnp.einsum('ksab,kcb->ksac', left_vals, partner_slot, preferred_element_t...]
    reshape x1 -> x0, other arithmetic: 1.46 us -> none  [on_device(): summed.astype(jnp.bfloat16).reshape(out_block.shape + x_vals.shape[3:])]
  transfers between devices with their start and end apart: 11 -> 0, of which waited for: 7 -> 0; matrix products, arithmetic and copies ran while one was open for 11% -> 0% of each run, Pallas kernels for 0% -> 0%
where the time goes in v1:
time: 22 us; the launch traced here: 21.8 us
  Pallas kernels  19.8 us (90%)
  local copies, waits for them, and re-layouts  1.38 us (6%)
  between operations  0.66 us (3%)
    pallas_call x1, Pallas kernels, on_device(): pl.pallas_call(functools.partial(kernel, sizes), out_shape=jax.ShapeDtype...  19.8 us
    unnamed x1, local copies, waits for them, and re-layouts  1.38 us

profile of v1, /device:TPU:0, one launch (start us, length us, event | category | flops | bytes accessed | tf_op | source)
XLA Modules:
  0.0 21.8 jit_solution(3641874999715220561)
XLA Ops:
  0.7 19.8 %shard_map.37 = bf16[1,1,1,128,128]{4,3,2,1,0:T(8,128)(2,1)} custom-call(s32[1,2,4]{2,1,0:T(2,128)} %rows_ref.1, s32[1,1,1]{2,1,0:T(1,128)S(6)} %copy.5.pos_ref, bf16[1,2,4,128,128]{4,3,2,1,0:T(8,128)(2,1)} %x_ref.1), custom_call_target="tpu_custom_call" | custom-call | tf_op jit(solution)/shard_map/pallas_call | solution.py:176
  20.4 1.4 %copy.6 = bf16[1,1,1,128,128]{4,3,2,1,0:T(8,128)(2,1)} copy(bf16[1,1,1,128,128]{4,3,2,1,0:T(8,128)(2,1)} %shard_map.37) | data formatting | bytes 65536
